TPU v7x, 256 devices: a whole 4x4x8 slice. The times are simulated.
256 devices in a mesh: section: 4 (over y), row: 8 (over z_hi, x), col: 8 (over z_lo, core).
Axes of the slice: x: 4, y: 4, z: 8 (z_hi: 2, z_lo: 4; z = z_hi * 4 + z_lo), core: 2. Of those that a mesh axis runs over, the one named last changes fastest.
Arguments:
- section_inputs: bfloat16 [4, 2048, 2048], P('section', 'col', 'row'), may hold values from -6 to 6
- out_grad: bfloat16 [4, 2048, 2048], P('section', 'col', 'row'), may hold values from -6 to 6
- saved_gate: bfloat16 [4, 2048, 8192], P('section', 'row', 'col'), may hold values from -6 to 6
- saved_up: bfloat16 [4, 2048, 8192], P('section', 'row', 'col'), may hold values from -6 to 6
- gate_weight: bfloat16 [4, 2048, 8192], P('section', 'row', 'col'), may hold values from -0.125 to 0.125
- up_weight: bfloat16 [4, 2048, 8192], P('section', 'row', 'col'), may hold values from -0.125 to 0.125
- down_weight: bfloat16 [4, 8192, 2048], P('section', 'col', 'row'), may hold values from -0.0625 to 0.0625
- momentum_gate: float32 [4, 2048, 8192], P('section', 'row', 'col'), may hold values from -6 to 6
- momentum_up: float32 [4, 2048, 8192], P('section', 'row', 'col'), may hold values from -6 to 6
- momentum_down: float32 [4, 8192, 2048], P('section', 'col', 'row'), may hold values from -6 to 6
- noise_gate: bfloat16 [4, 2048, 8192], P('section', 'row', 'col'), may hold values from -6 to 6
- noise_up: bfloat16 [4, 2048, 8192], P('section', 'row', 'col'), may hold values from -6 to 6
- noise_down: bfloat16 [4, 8192, 2048], P('section', 'col', 'row'), may hold values from -6 to 6
Outputs:
- prev_grads: bfloat16 [4, 2048, 2048], P('section', 'col', 'row')
- new_gate: bfloat16 [4, 2048, 8192], P('section', 'row', 'col')
- new_up: bfloat16 [4, 2048, 8192], P('section', 'row', 'col')
- new_down: bfloat16 [4, 8192, 2048], P('section', 'col', 'row')
- next_momentum_gate: float32 [4, 2048, 8192], P('section', 'row', 'col')
- next_momentum_up: float32 [4, 2048, 8192], P('section', 'row', 'col')
- next_momentum_down: float32 [4, 8192, 2048], P('section', 'col', 'row')
All inputs are finite; a program needn't handle non-finite values.
Results may differ from a plain program's by a relative error of at most 0.025.
Values may be sent and summed in bfloat16 or wider, within the bound.
A program may use at most 128 MiB of HBM per device.

v0:
```python
import jax
import jax.numpy as jnp
from jax import lax
from jax.sharding import PartitionSpec as P

FRICTION = 0.1
DRIFT = 0.01


def from_behind(shard, axis, by):
    size = lax.axis_size(axis)
    pairs = [(i, i + by) for i in range(size) if 0 <= i + by < size]
    return lax.ppermute(shard, axis, pairs)


def contract(left, right, left_dim, right_dim):
    return lax.dot_general(
        left, right, (((left_dim,), (right_dim,)), ((), ())), preferred_element_type=jnp.float32
    )


def pre_grads(hidden_grad, gate_pre, up_pre):
    gate_wide = gate_pre.astype(jnp.float32)
    up_wide = up_pre.astype(jnp.float32)
    sigmoid_gate = jax.nn.sigmoid(gate_wide)
    silu_gate = gate_wide * sigmoid_gate
    slope = sigmoid_gate * (1.0 + gate_wide * (1.0 - sigmoid_gate))
    gate_grad = (hidden_grad * up_wide * slope).astype(jnp.bfloat16)
    up_grad = (hidden_grad * silu_gate).astype(jnp.bfloat16)
    hidden_saved = (silu_gate * up_wide).astype(jnp.bfloat16)
    return (hidden_saved, gate_grad, up_grad)


def sghmc_step(weight, momentum, gradient, noise, kick_scale):
    moved = (
        (1.0 - FRICTION) * momentum
        - kick_scale * gradient
        + (2.0 * FRICTION) ** 0.5 * noise.astype(jnp.float32)
    )
    fresh = (weight.astype(jnp.float32) + DRIFT * moved).astype(jnp.bfloat16)
    return (fresh[None], moved[None])


def shards(
    section_inputs,
    out_grad,
    saved_gate,
    saved_up,
    gate_weight,
    up_weight,
    down_weight,
    momentum_gate,
    momentum_up,
    momentum_down,
    noise_gate,
    noise_up,
    noise_down,
):
    inputs_full, grads_full = (
        lax.all_gather(section_inputs[0], "col", axis=0, tiled=True),
        lax.all_gather(out_grad[0], "col", axis=0, tiled=True),
    )
    tokens = inputs_full.shape[0]
    gate_local = gate_weight[0]
    up_local = up_weight[0]
    down_local = down_weight[0]
    grad_block = grads_full
    hidden_grad = lax.psum_scatter(
        contract(grad_block, down_local, 1, 1).astype(jnp.bfloat16),
        "row",
        scatter_dimension=0,
        tiled=True,
    ).astype(jnp.float32)
    hidden_saved, gate_grad, up_grad = pre_grads(hidden_grad, saved_gate[0], saved_up[0])
    hidden_piece = lax.all_gather(hidden_saved, "row", axis=0, tiled=True)
    gate_piece = lax.all_gather(gate_grad, "row", axis=0, tiled=True)
    up_piece = lax.all_gather(up_grad, "row", axis=0, tiled=True)
    grad_block = grads_full
    down_total = contract(hidden_piece, grad_block, 0, 0)
    gate_total = contract(inputs_full, gate_piece, 0, 0)
    up_total = contract(inputs_full, up_piece, 0, 0)
    partial_value = contract(gate_piece, gate_local, 1, 1) + contract(up_piece, up_local, 1, 1)
    input_part = partial_value
    down_wgrad, gate_wgrad, up_wgrad, input_part = (down_total, gate_total, up_total, input_part)
    input_grad = lax.psum_scatter(
        input_part.astype(jnp.bfloat16), "col", scatter_dimension=0, tiled=True
    )
    passed = from_behind(input_grad, "section", -1)
    kick_scale = float(tokens) ** (-0.5)
    new_gate, next_gate = sghmc_step(
        gate_local, momentum_gate[0], gate_wgrad, noise_gate[0], kick_scale
    )
    new_up, next_up = sghmc_step(up_local, momentum_up[0], up_wgrad, noise_up[0], kick_scale)
    new_down, next_down = sghmc_step(
        down_local, momentum_down[0], down_wgrad, noise_down[0], kick_scale
    )
    return (passed[None], new_gate, new_up, new_down, next_gate, next_up, next_down)


def solution(mesh):
    in_specs = (
        P("section", "col", "row"),
        P("section", "col", "row"),
        P("section", "row", "col"),
        P("section", "row", "col"),
        P("section", "row", "col"),
        P("section", "row", "col"),
        P("section", "col", "row"),
        P("section", "row", "col"),
        P("section", "row", "col"),
        P("section", "col", "row"),
        P("section", "row", "col"),
        P("section", "row", "col"),
        P("section", "col", "row"),
    )
    out_specs = (
        P("section", "col", "row"),
        P("section", "row", "col"),
        P("section", "row", "col"),
        P("section", "col", "row"),
        P("section", "row", "col"),
        P("section", "row", "col"),
        P("section", "col", "row"),
    )
    return jax.shard_map(shards, mesh=mesh, in_specs=in_specs, out_specs=out_specs, check_vma=False)
```

profile of v0, /device:TPU:8, one launch (start us, length us, event | category | flops | bytes accessed | tf_op | source)
XLA Modules:
  0.0 585.1 jit_solution(10112949848382311363)
XLA Ops:
  7.2 0.7 all-gather.14.cloned.1.call-update
  7.9 42.1 %all-gather.14.cloned.1.call-done = bf16[1,2048,256]{2,1,0:T(8,128)(2,1)} async-done(((bf16[1,256,256]{2,1,0:T(8,128)(2,1)}), bf16[1,2048,256]{2,1,0:T(8,128)(2,1)}) %all-gather.14.cloned.1.call-update) | async-done | bytes 1048592 | tf_op jit(solution)/shard_map/all_gather | solution.py:61
  50.0 4.6 convolution_convert_fusion
  54.8 125.2 %reduce-scatter.3.cloned.1.call-done = bf16[256,1024]{1,0:T(8,128)(2,1)} async-done(((bf16[2048,1024]{1,0:T(8,128)(2,1)}), bf16[256,1024]{1,0:T(8,128)(2,1)}) %reduce-scatter.3.cloned.1.call-update) | async-done | bytes 524304 | tf_op jit(solution)/shard_map/reduce_scatter | solution.py:68
  180.0 3.0 fusion.12
  183.0 0.5 all-gather.10.cloned.1.call-update
  183.6 0.5 all-gather.12.cloned.1.call-update
  184.8 1.0 copy.23
  185.8 1.0 copy.25
  186.8 1.2 copy.20
  188.0 1.2 copy.21
  189.3 1.3 copy.22
  190.6 1.3 copy.24
  191.9 93.9 %all-gather.8.cloned.1.call-done = bf16[2048,1024]{1,0:T(8,128)(2,1)} async-done(((bf16[256,1024]{1,0:T(8,128)(2,1)}), bf16[2048,1024]{1,0:T(8,128)(2,1)}) %all-gather.8.cloned.1.call-update) | async-done | bytes 4194320 | tf_op jit(solution)/shard_map/all_gather | solution.py:76
  285.8 4.9 fusion.26
  290.7 99.9 %all-gather.10.cloned.1.call-done = bf16[2048,1024]{1,0:T(8,128)(2,1)} async-done(((bf16[256,1024]{1,0:T(8,128)(2,1)}), bf16[2048,1024]{1,0:T(8,128)(2,1)}) %all-gather.10.cloned.1.call-update) | async-done | bytes 4194320 | tf_op jit(solution)/shard_map/all_gather | solution.py:77
  390.6 5.1 fusion
  395.7 99.6 %all-gather.12.cloned.1.call-done = bf16[2048,1024]{1,0:T(8,128)(2,1)} async-done(((bf16[256,1024]{1,0:T(8,128)(2,1)}), bf16[2048,1024]{1,0:T(8,128)(2,1)}) %all-gather.12.cloned.1.call-update) | async-done | bytes 4194320 | tf_op jit(solution)/shard_map/all_gather | solution.py:75
  495.3 3.9 fusion.8
  499.3 1.0 copy-done.4
  500.2 1.0 fusion.24
  501.2 27.8 %all-gather.16.cloned.1.call-done = bf16[1,2048,256]{2,1,0:T(8,128)(2,1)} async-done(((bf16[1,256,256]{2,1,0:T(8,128)(2,1)}), bf16[1,2048,256]{2,1,0:T(8,128)(2,1)}) %all-gather.16.cloned.1.call-update) | async-done | bytes 1048592 | tf_op jit(solution)/shard_map/all_gather | solution.py:60
  529.0 4.2 fusion.4
  533.8 1.3 fusion.6
  535.1 33.2 %reduce-scatter.5.cloned.1.call-done = bf16[256,256]{1,0:T(8,128)(2,1)} async-done(((bf16[2048,256]{1,0:T(8,128)(2,1)}), bf16[256,256]{1,0:T(8,128)(2,1)}) %reduce-scatter.5.cloned.1.call-update) | async-done | bytes 131088 | tf_op jit(solution)/shard_map/reduce_scatter | solution.py:85
  568.2 2.7 collective-permute-start
  571.0 0.9 fusion.23
  571.9 1.0 copy.26
  572.9 2.0 copy.27
  574.9 1.3 copy.29
  576.2 1.3 copy.28
  577.6 0.7 copy.31
  (42 shorter events, 1.4 us)
Async XLA Ops:
  7.2 42.9 %all-gather.14.cloned.1.call-start = ((), (), s32[]{:S(2)}) async-start(), calls=%async_computation.7 | async-start | bytes 1179648 | tf_op jit(solution)/shard_map/all_gather | solution.py:61
  7.9 172.1 %reduce-scatter.3.cloned.1.call-start = ((), (), s32[]{:S(2)}) async-start(), calls=%async_computation.2 | async-start | bytes 4718592 | tf_op jit(solution)/shard_map/reduce_scatter | solution.py:68
  54.7 125.3 %copy-start.11 = (bf16[1,256,1024]{2,1,0:T(8,128)(2,1)S(1)}, bf16[1,256,1024]{2,1,0:T(8,128)(2,1)}, u32[]{:S(2)}) copy-start(bf16[1,256,1024]{2,1,0:T(8,128)(2,1)} %param.16) | copy-start | bytes 1572868
  54.7 125.3 %copy-start.12 = (bf16[1,256,1024]{2,1,0:T(8,128)(2,1)S(1)}, bf16[1,256,1024]{2,1,0:T(8,128)(2,1)}, u32[]{:S(2)}) copy-start(bf16[1,256,1024]{2,1,0:T(8,128)(2,1)} %param.15) | copy-start | bytes 1572868
  54.7 130.1 %copy-start.6 = (bf16[1,256,1024]{2,1,0:T(8,128)(2,1)S(1)}, bf16[1,256,1024]{2,1,0:T(8,128)(2,1)}, u32[]{:S(2)}) copy-start(bf16[1,256,1024]{2,1,0:T(8,128)(2,1)} %param.23) | copy-start | bytes 1572868
  54.7 131.1 %copy-start.7 = (bf16[1,256,1024]{2,1,0:T(8,128)(2,1)S(1)}, bf16[1,256,1024]{2,1,0:T(8,128)(2,1)}, u32[]{:S(2)}) copy-start(bf16[1,256,1024]{2,1,0:T(8,128)(2,1)} %param.24) | copy-start | bytes 1572868
  54.7 134.6 %copy-start.2 = (f32[1,256,1024]{2,1,0:T(8,128)S(1)}, f32[1,256,1024]{2,1,0:T(8,128)}, u32[]{:S(2)}) copy-start(f32[1,256,1024]{2,1,0:T(8,128)} %param.20) | copy-start | bytes 3145732
  54.7 231.1 %all-gather.8.cloned.1.call-start = ((), (), s32[]{:S(2)}) async-start(), calls=%async_computation.3 | async-start | bytes 4718592 | tf_op jit(solution)/shard_map/all_gather | solution.py:76
  182.9 7.7 %copy-start.3 = (f32[1,256,1024]{2,1,0:T(8,128)S(1)}, f32[1,256,1024]{2,1,0:T(8,128)}, u32[]{:S(2)}) copy-start(f32[1,256,1024]{2,1,0:T(8,128)} %param.21) | copy-start | bytes 3145732
  183.0 207.6 %all-gather.10.cloned.1.call-start = ((), (), s32[]{:S(2)}) async-start(), calls=%async_computation.4 | async-start | bytes 4718592 | tf_op jit(solution)/shard_map/all_gather | solution.py:77
  183.5 311.8 %all-gather.12.cloned.1.call-start = ((), (), s32[]{:S(2)}) async-start(), calls=%async_computation.6 | async-start | bytes 4718592 | tf_op jit(solution)/shard_map/all_gather | solution.py:75
  184.1 344.8 %all-gather.16.cloned.1.call-start = ((), (), s32[]{:S(2)}) async-start(), calls=%async_computation.8 | async-start | bytes 1179648 | tf_op jit(solution)/shard_map/all_gather | solution.py:60
  184.7 383.5 %reduce-scatter.5.cloned.1.call-start = ((), (), s32[]{:S(2)}) async-start(), calls=%async_computation.5 | async-start | bytes 1179648 | tf_op jit(solution)/shard_map/reduce_scatter | solution.py:85
  191.9 198.6 %copy-start.8 = (bf16[1,256,1024]{2,1,0:T(8,128)(2,1)S(1)}, bf16[1,256,1024]{2,1,0:T(8,128)(2,1)}, u32[]{:S(2)}) copy-start(bf16[1,256,1024]{2,1,0:T(8,128)(2,1)} %param.18) | copy-start | bytes 1572868
  290.7 204.6 %copy-start = (bf16[1,2048,256]{2,1,0:T(8,128)(2,1)S(1)}, bf16[1,2048,256]{2,1,0:T(8,128)(2,1)}, u32[]{:S(2)}) copy-start(bf16[1,2048,256]{2,1,0:T(8,128)(2,1)} %all-gather.14.cloned.1.call-done) | copy-start | bytes 3145732
  395.7 104.5 %copy-start.1 = (bf16[1,1024,256]{2,1,0:T(8,128)(2,1)S(1)}, bf16[1,1024,256]{2,1,0:T(8,128)(2,1)}, u32[]{:S(2)}) copy-start(bf16[1,1024,256]{2,1,0:T(8,128)(2,1)} %param.19) | copy-start | bytes 1572868
  395.7 133.2 %copy-start.10 = (bf16[1,256,1024]{1,2,0:T(8,128)(2,1)S(1)}, bf16[1,256,1024]{1,2,0:T(8,128)(2,1)}, u32[]{:S(2)}) copy-start(bf16[1,256,1024]{1,2,0:T(8,128)(2,1)} %copy.23) | copy-start | bytes 1572868
  499.3 1.0 copy-start.4
  529.0 4.4 copy-start.5
  529.0 4.4 copy-start.9
  529.0 4.5 copy-start.13
  529.0 4.8 copy-start.14
  568.2 9.3 %collective-permute-start = (bf16[256,256]{1,0:T(8,128)(2,1)}, bf16[256,256]{1,0:T(8,128)(2,1)S(1)}, u32[]{:S(2)}, u32[]{:S(2)}) collective-permute-start(bf16[256,256]{1,0:T(8,128)(2,1)} %reduce-scatter.5.cloned.1.call-done), channel_id=1, source_target_pairs={{64,0},{128,64},{192,128},{65,1},{129,65},{193,129},{66,2},{130,66... | collective-permute-start | bytes 393224 | tf_op jit(solution)/shard_map/ppermute | solution.py:13
Sparse Core Ops, SparseCore 0:
  9.8 40.2 all-gather.13
  54.8 125.1 reduce-scatter.2
  183.2 102.5 all-gather.7
  288.9 101.6 all-gather.9
  393.6 101.6 all-gather.11
  496.9 31.9 all-gather.15
  532.1 36.1 reduce-scatter.4
where the time goes:
time: 585 us
  waiting for transfers between devices  524 us (90%)
  matrix products  24.1 us (4%)
  local copies, waits for them, and re-layouts  14.8 us (3%)
  between operations  14.3 us (2%)
    reduce_scatter x1, waiting for transfers between devices, shards(): lax.psum_scatter(contract(grad_block, down_local, 1, 1).astype(jnp.bfloat...  125 us
    all_gather x1, waiting for transfers between devices, shards(): up_piece = lax.all_gather(up_grad, 'row', axis=0, tiled=True)  99.9 us
    all_gather x1, waiting for transfers between devices, shards(): hidden_piece = lax.all_gather(hidden_saved, 'row', axis=0, tiled=True)  99.6 us
    all_gather x1, waiting for transfers between devices, shards(): gate_piece = lax.all_gather(gate_grad, 'row', axis=0, tiled=True)  93.9 us
    all_gather x1, waiting for transfers between devices, shards(): lax.all_gather(out_grad[0], 'col', axis=0, tiled=True)  42.1 us
    reduce_scatter x1, waiting for transfers between devices, shards(): lax.psum_scatter(input_part.astype(jnp.bfloat16), 'col', scatter_dimensio...  33.2 us
    all_gather x1, waiting for transfers between devices, shards(): lax.all_gather(section_inputs[0], 'col', axis=0, tiled=True)  27.8 us
    dot_general x6, matrix products, contract(): lax.dot_general(left, right, (((left_dim,), (right_dim,)), ((), ())), pre...  24.1 us
  transfers between devices with their start and end apart: 8, of which 7 were waited for; matrix products, arithmetic and copies ran while one was open for 6% of the time, Pallas kernels for 0%

commit v1 on v0

v1 whole, which is shorter than its diff:
```python
import functools

import jax
import jax.numpy as jnp
from jax import lax
from jax.experimental import pallas as pl
from jax.experimental.pallas import tpu as pltpu
from jax.sharding import PartitionSpec as P

FRICTION = 0.1
DRIFT = 0.01
MESH = pl.DeviceIdType.MESH
BF = jnp.bfloat16
F32 = jnp.float32
NC = 4

DN, SGX, SUX, GTX, UPX = 0, NC, 2 * NC, 3 * NC, 4 * NC
DYR = 5 * NC
DYC = DYR + 8
XR = DYC + 8
XC = XR + 8
RS = XC + 8
AG = RS + 3 * NC
AF = AG + 6 * NC
WX = AF + 6 * NC
DXC = WX + 3 * NC
DXR = DXC + 4
FIN = DXR + 8
NSEM = FIN + 1


def nt(a, b):
    return lax.dot_general(a, b, (((1,), (1,)), ((), ())), preferred_element_type=F32)


def nn(a, b):
    return jnp.dot(a, b, preferred_element_type=F32)


def kernel(
    kick,
    x_in, dy_in, sg_in, su_in, wg_in, wu_in, wd_in, mg_in, mu_in, md_in, ng_in, nu_in, nd_in,
    prev_out, wg_out, wu_out, wd_out, mg_out, mu_out, md_out,
    x_stage, dyf, xt, down_f, gate_f, up_f, sg_f, su_f, hgs, rsr, ht, g, u,
    wds, wgs, wus, wdr, wgr, wur, mg, mu, md, ng, nu, nd, wg, wu, wd,
    acc, dxs, dxr, psend, precv, fin, finr, outv,
    ssem, rsem, lsem, osem,
):
    tb, fb = x_in.shape[1], x_in.shape[2]
    half = sg_in.shape[2] // 2
    cw = half // NC
    xb = 2 * tb

    y, row, col = lax.axis_index("section"), lax.axis_index("row"), lax.axis_index("col")
    zh, x, zl, core = row // 4, row % 4, col // 2, col % 2
    z = zh * 4 + zl
    oh = 1 - zh

    def at_z(zz):
        return (y, (zz // 4) * 4 + x, (zz % 4) * 2 + core)

    def at_x(xx):
        return (y, zh * 4 + xx, col)

    partner = (y, oh * 4 + x, col)
    z_next, z_prev = at_z((z + 1) % 8), at_z((z + 7) % 8)
    x1, x2, x3 = (x + 1) % 4, (x + 2) % 4, (x + 3) % 4
    x_next, x_prev, x_far = at_x(x1), at_x(x3), at_x(x2)
    twin = (y, row, zl * 2 + 1 - core)
    y_prev, y_next = ((y + 3) % 4, row, col), ((y + 1) % 4, row, col)

    def rcopy(src, dst, sem, to):
        return pltpu.make_async_remote_copy(
            src_ref=src, dst_ref=dst, send_sem=ssem.at[sem], recv_sem=rsem.at[sem],
            device_id=to, device_id_type=MESH,
        )

    def send(src, dst, sem, to):
        rcopy(src, dst, sem, to).start()

    def got(dst, sem):
        rcopy(dst, dst, sem, partner).wait_recv()

    def sent(src, sem):
        rcopy(src, src, sem, partner).wait_send()

    def cols(at, j):
        return pl.ds(pl.multiple_of(at * half + j * cw, cw), cw)

    def chunk(j):
        return pl.ds(pl.multiple_of(j * cw, cw), cw)

    def place(zz, kk):
        return ((((zz % 2) * 2 + kk) * 2) + (zz % 4) // 2) * tb

    def dy_slot(zz, kk, first=0, size=tb):
        return dyf.at[zz // 4, pl.ds(pl.multiple_of(place(zz, kk) + first, 16), size)]

    def x_slot(zz, kk, first=0, size=fb):
        return xt.at[zz // 4, pl.ds(first, size), pl.ds(pl.multiple_of(place(zz, kk), tb), tb)]

    bar = pltpu.get_barrier_semaphore()
    for to in (partner, z_next, z_prev, x_next, x_prev, x_far, twin, y_next):
        pl.semaphore_signal(bar, inc=1, device_id=to, device_id_type=MESH)

    own_half = pl.ds(pl.multiple_of(zh * half, half), half)
    loads = [
        pltpu.make_async_copy(s, d, lsem.at[i])
        for i, (s, d) in enumerate([
            (x_in.at[0], x_stage),
            (dy_in.at[0], dy_slot(z, core)),
            (wd_in.at[0, own_half], down_f.at[zh]),
            (sg_in.at[0, :, own_half], sg_f.at[zh]),
            (su_in.at[0, :, own_half], su_f.at[zh]),
            (wg_in.at[0, :, own_half], gate_f.at[zh]),
            (wu_in.at[0, :, own_half], up_f.at[zh]),
            (mg_in.at[0], mg), (mu_in.at[0], mu), (md_in.at[0], md),
            (ng_in.at[0], ng), (nu_in.at[0], nu), (nd_in.at[0], nd),
            (wg_in.at[0], wg), (wu_in.at[0], wu), (wd_in.at[0], wd),
        ])
    ]
    for load in loads:
        load.start()
    pl.semaphore_wait(bar, 8)

    def ring(slot, base, cbase, step):
        size = tb if slot is dy_slot else fb
        back, ahead = (z + 8 - step) % 8, (z + step) % 8
        if step < 3:
            send(slot(back, core), slot(back, core), base + 2 * step, z_next)
            send(slot(ahead, core), slot(ahead, core), base + 2 * step + 1, z_prev)
        elif step == 3:
            lo, hi = (0, size // 2), (size // 2, size // 2)
            send(slot(back, core, *lo), slot(back, core, *lo), base + 6, z_next)
            send(slot(ahead, core, *hi), slot(ahead, core, *hi), base + 7, z_prev)
        if step == 0 or step == 4:
            send(slot(back, core), slot(back, core), cbase + 2 * step - (step == 4), twin)
        else:
            send(slot(back, core), slot(back, core), cbase + 2 * step - 1, twin)
            send(slot(ahead, core), slot(ahead, core), cbase + 2 * step, twin)

    def ring_got(slot, base, step):
        size = tb if slot is dy_slot else fb
        back, ahead = (z + 8 - step) % 8, (z + step) % 8
        if step < 4:
            got(slot(back, core), base + 2 * step - 2)
            got(slot(ahead, core), base + 2 * step - 1)
        else:
            got(slot(back, core, 0, size // 2), base + 6)
            got(slot(ahead, core, size // 2, size // 2), base + 7)

    def ring_order():
        return [(0, z)] + [
            (2 * s - 1 + d, (z + 8 - s) % 8 if d == 0 else (z + s) % 8) for s in (1, 2, 3) for d in (0, 1)
        ] + [(7, (z + 4) % 8)]

    def ring_sent(slot, base, cbase):
        size = tb if slot is dy_slot else fb
        for step in range(3):
            sent(slot(z, core), base + 2 * step)
            sent(slot(z, core), base + 2 * step + 1)
        sent(slot(z, core, 0, size // 2), base + 6)
        sent(slot(z, core, 0, size // 2), base + 7)
        for i in range(8):
            sent(slot(z, core), cbase + i)

    loads[1].wait()
    ring(dy_slot, DYR, DYC, 0)

    @pl.loop(0, NC)
    def _(j):
        there = pl.ds(pl.multiple_of(oh * half + j * cw, cw), cw)
        send(wd_in.at[0, there], down_f.at[zh, chunk(j)], DN + j, partner)

    loads[0].wait()
    x_slot_own = x_slot(z, core)
    x_slot_own[...] = x_stage[...].astype(F32).T.astype(BF)
    acc[...] = jnp.zeros_like(acc)

    for step in (1, 2, 3):
        ring_got(dy_slot, DYR, step)
        ring(dy_slot, DYR, DYC, step)

    @pl.loop(0, NC)
    def _(j):
        send(sg_in.at[0, :, cols(oh, j)], sg_f.at[zh, :, chunk(j)], SGX + j, partner)
        send(su_in.at[0, :, cols(oh, j)], su_f.at[zh, :, chunk(j)], SUX + j, partner)

    ring_got(dy_slot, DYR, 4)
    ring(dy_slot, DYR, DYC, 4)
    loads[2].wait()
    for i, zz in ring_order():
        got(dy_slot(zz, 1 - core), DYC + i)

    def partial_hidden(j):
        got(down_f.at[oh, chunk(j)], DN + j)

        @pl.loop(0, 4)
        def _(xx):
            rows = pl.ds(pl.multiple_of(xx * xb, xb), xb)
            hgs[j, xx] = (
                nt(dyf[0, rows, :], down_f[0, chunk(j), :]) + nt(dyf[1, rows, :], down_f[1, chunk(j), :])
            ).astype(BF)

        send(hgs.at[j, x1], rsr.at[j, 0], RS + 3 * j, x_next)
        send(hgs.at[j, x2], rsr.at[j, 1], RS + 3 * j + 1, x_far)
        send(hgs.at[j, x3], rsr.at[j, 2], RS + 3 * j + 2, x_prev)

    ring(x_slot, XR, XC, 0)
    pl.loop(0, NC)(partial_hidden)

    @pl.loop(0, NC)
    def _(j):
        send(wg_in.at[0, :, cols(oh, j)], gate_f.at[zh, :, chunk(j)], GTX + j, partner)
        send(wu_in.at[0, :, cols(oh, j)], up_f.at[zh, :, chunk(j)], UPX + j, partner)

    for step in (1, 2, 3):
        ring_got(x_slot, XR, step)
        ring(x_slot, XR, XC, step)
    for i in (3, 4, 5, 6):
        loads[i].wait()

    def activations(j):
        for d in range(3):
            got(rsr.at[j, d], RS + 3 * j + d)
        got(sg_f.at[oh, :, chunk(j)], SGX + j)
        got(su_f.at[oh, :, chunk(j)], SUX + j)
        for part in range(2):
            rows = pl.ds(part * tb, tb)
            hidden_grad = hgs[j, x, rows, :].astype(F32)
            for d in range(3):
                hidden_grad = hidden_grad + rsr[j, d, rows, :].astype(F32)
            gate_pre = sg_f[part, :, chunk(j)].astype(F32)
            up_pre = su_f[part, :, chunk(j)].astype(F32)
            sigmoid_gate = jax.nn.sigmoid(gate_pre)
            silu_gate = gate_pre * sigmoid_gate
            slope = sigmoid_gate * (1.0 + gate_pre * (1.0 - sigmoid_gate))
            g[j, x, rows, :] = (hidden_grad * up_pre * slope).astype(BF)
            u[j, x, rows, :] = (hidden_grad * silu_gate).astype(BF)
            ht[j, x, :, rows] = (silu_gate * up_pre).T.astype(BF)
        for i, ref in enumerate((ht, g, u)):
            send(ref.at[j, x], ref.at[j, x], AG + 6 * j + i, x_next)
            send(ref.at[j, x], ref.at[j, x], AG + 6 * j + 3 + i, x_prev)

    def halves(ref, j, xx, second):
        size = ref.shape[2] // 2
        return ref.at[j, xx, pl.ds(second * size, size)]

    def forward(j):
        for i, ref in enumerate((ht, g, u)):
            got(ref.at[j, x3], AG + 6 * j + i)
            send(halves(ref, j, x3, 0), halves(ref, j, x3, 0), AF + 6 * j + i, x_next)
            got(ref.at[j, x1], AG + 6 * j + 3 + i)
            send(halves(ref, j, x1, 1), halves(ref, j, x1, 1), AF + 6 * j + 3 + i, x_prev)

    def step_columns(i, w, m, n, w_out, m_out, at, j, grad):
        c = cols(at, j)
        moved = (1.0 - FRICTION) * m[:, c] - kick * grad + (2.0 * FRICTION) ** 0.5 * n[:, c].astype(F32)
        m[:, c] = moved
        w[:, c] = (w[:, c].astype(F32) + DRIFT * moved).astype(BF)
        pltpu.make_async_copy(m.at[:, c], m_out.at[0, :, c], osem.at[at, j, 2 * i]).start()
        pltpu.make_async_copy(w.at[:, c], w_out.at[0, :, c], osem.at[at, j, 2 * i + 1]).start()

    def step_rows(at, j, grad):
        c = cols(at, j)
        moved = (1.0 - FRICTION) * md[c, :] - kick * grad + (2.0 * FRICTION) ** 0.5 * nd[c, :].astype(F32)
        md[c, :] = moved
        wd[c, :] = (wd[c, :].astype(F32) + DRIFT * moved).astype(BF)
        pltpu.make_async_copy(md.at[c, :], md_out.at[0, c, :], osem.at[at, j, 4]).start()
        pltpu.make_async_copy(wd.at[c, :], wd_out.at[0, c, :], osem.at[at, j, 5]).start()

    def weight_grads(j):
        for i, ref in enumerate((ht, g, u)):
            got(halves(ref, j, x2, 0), AF + 6 * j + i)
            got(halves(ref, j, x2, 1), AF + 6 * j + 3 + i)

        def down_grad(at):
            total = nn(ht[j, 0], dyf[at, pl.ds(0, xb), :])
            for xx in range(1, 4):
                total = total + nn(ht[j, xx], dyf[at, pl.ds(xx * xb, xb), :])
            return total

        def column_grad(at, ref):
            total = nn(xt[at, :, pl.ds(0, xb)], ref[j, 0])
            for xx in range(1, 4):
                total = total + nn(xt[at, :, pl.ds(xx * xb, xb)], ref[j, xx])
            return total

        wds[j] = down_grad(oh).astype(BF)
        send(wds.at[j], wdr.at[j], WX + 3 * j, partner)
        wgs[j] = column_grad(oh, g).astype(BF)
        send(wgs.at[j], wgr.at[j], WX + 3 * j + 1, partner)
        wus[j] = column_grad(oh, u).astype(BF)
        send(wus.at[j], wur.at[j], WX + 3 * j + 2, partner)

        got(gate_f.at[oh, :, chunk(j)], GTX + j)
        got(up_f.at[oh, :, chunk(j)], UPX + j)

        @pl.loop(0, 4)
        def _(xx):
            rows = pl.ds(pl.multiple_of(xx * xb, xb), xb)
            for at in range(2):
                acc[at, rows, :] += nt(g[j, xx], gate_f[at, :, chunk(j)]) + nt(u[j, xx], up_f[at, :, chunk(j)])

        step_rows(zh, j, down_grad(zh))
        step_columns(0, wg, mg, ng, wg_out, mg_out, zh, j, column_grad(zh, g))
        step_columns(1, wu, mu, nu, wu_out, mu_out, zh, j, column_grad(zh, u))

    def partner_grads(j):
        got(wdr.at[j], WX + 3 * j)
        step_rows(oh, j, wdr[j].astype(F32))
        got(wgr.at[j], WX + 3 * j + 1)
        step_columns(0, wg, mg, ng, wg_out, mg_out, oh, j, wgr[j].astype(F32))
        got(wur.at[j], WX + 3 * j + 2)
        step_columns(1, wu, mu, nu, wu_out, mu_out, oh, j, wur[j].astype(F32))

    activations(0)
    ring_got(x_slot, XR, 4)
    ring(x_slot, XR, XC, 4)
    for i, zz in ring_order():
        got(x_slot(zz, 1 - core), XC + i)
    for i in range(7, 16):
        loads[i].wait()

    @pl.loop(1, NC + 2)
    def _(i):
        @pl.when(i < NC)
        def _():
            activations(i)

        @pl.when(i <= NC)
        def _():
            forward(i - 1)

        @pl.when(i >= 2)
        def _():
            weight_grads(i - 2)

    for m in range(2):
        for at in range(2):
            rows = pl.ds(pl.multiple_of((1 - core + 2 * m) * xb, xb), xb)
            dxs[at, m] = acc[at, rows, :].astype(BF)
            send(dxs.at[at, m], dxr.at[at, m], DXC + 2 * m + at, twin)
    for m in range(2):
        for at in range(2):
            got(dxr.at[at, m], DXC + 2 * m + at)

    def part(zz, first=0, size=tb):
        at, late, m = zz // 4, (zz % 4) // 2, zz % 2
        mine = pl.ds(pl.multiple_of(((core + 2 * m) * 2 + late) * tb + first, 16), size)
        other = pl.ds(pl.multiple_of(late * tb + first, 16), size)
        return acc[at, mine, :] + dxr[at, m, other, :].astype(F32)

    ht2 = tb // 2
    far = (z + 4) % 8
    psend[0, 0, pl.ds(0, ht2), :] = part(far, 0, ht2).astype(BF)
    send(psend.at[0, 0, pl.ds(0, ht2)], precv.at[0, 0, pl.ds(0, ht2)], DXR, z_next)
    psend[1, 0, pl.ds(0, ht2), :] = part(far, ht2, ht2).astype(BF)
    send(psend.at[1, 0, pl.ds(0, ht2)], precv.at[1, 0, pl.ds(0, ht2)], DXR + 1, z_prev)
    for step in (1, 2, 3):
        for d in range(2):
            to = (z + 4 - step) % 8 if d == 0 else (z + 4 + step) % 8
            if step == 1:
                got(precv.at[d, 0, pl.ds(0, ht2)], DXR + d)
                psend[d, 1, pl.ds((1 - d) * ht2, ht2), :] = part(to, (1 - d) * ht2, ht2).astype(BF)
                psend[d, 1, pl.ds(d * ht2, ht2), :] = (
                    part(to, d * ht2, ht2) + precv[d, 0, pl.ds(0, ht2), :].astype(F32)
                ).astype(BF)
            else:
                got(precv.at[d, step - 1], DXR + 2 * (step - 1) + d)
                psend[d, step] = (part(to) + precv[d, step - 1].astype(F32)).astype(BF)
            send(psend.at[d, step], precv.at[d, step], DXR + 2 * step + d, z_next if d == 0 else z_prev)

    pl.loop(0, NC)(partner_grads)

    got(precv.at[0, 3], DXR + 6)
    got(precv.at[1, 3], DXR + 7)
    fin[...] = (part(z) + precv[0, 3].astype(F32) + precv[1, 3].astype(F32)).astype(BF)
    send(fin, finr, FIN, y_prev)
    got(finr, FIN)
    outv[...] = jnp.where(y == 3, jnp.zeros_like(finr), finr[...])
    last = pltpu.make_async_copy(outv, prev_out.at[0], lsem.at[0])
    last.start()

    ring_sent(dy_slot, DYR, DYC)
    ring_sent(x_slot, XR, XC)

    @pl.loop(0, NC)
    def _(j):
        sent(down_f.at[0, chunk(j)], DN + j)
        for ref, base in ((sg_f, SGX), (su_f, SUX), (gate_f, GTX), (up_f, UPX)):
            sent(ref.at[0, :, chunk(j)], base + j)
        for d in range(3):
            sent(rsr.at[j, d], RS + 3 * j + d)
        for i, ref in enumerate((ht, g, u)):
            for d in range(2):
                sent(ref.at[j, 0], AG + 6 * j + 3 * d + i)
                sent(halves(ref, j, 0, 0), AF + 6 * j + 3 * d + i)
        for i, ref in enumerate((wds, wgs, wus)):
            sent(ref.at[j], WX + 3 * j + i)
        for at in range(2):
            c = cols(at, j)
            for i, (w, m, w_out, m_out) in enumerate(((wg, mg, wg_out, mg_out), (wu, mu, wu_out, mu_out))):
                pltpu.make_async_copy(m.at[:, c], m_out.at[0, :, c], osem.at[at, j, 2 * i]).wait()
                pltpu.make_async_copy(w.at[:, c], w_out.at[0, :, c], osem.at[at, j, 2 * i + 1]).wait()
            pltpu.make_async_copy(md.at[c, :], md_out.at[0, c, :], osem.at[at, j, 4]).wait()
            pltpu.make_async_copy(wd.at[c, :], wd_out.at[0, c, :], osem.at[at, j, 5]).wait()

    for i in range(4):
        sent(dxs.at[0, 0], DXC + i)
    for d in range(2):
        sent(psend.at[d, 0, pl.ds(0, ht2)], DXR + d)
        for step in (1, 2, 3):
            sent(psend.at[d, step], DXR + 2 * step + d)
    sent(fin, FIN)
    last.wait()


def shards(*args):
    x_in, sg_in, wd_in = args[0], args[2], args[6]
    tb, fb = x_in.shape[1], x_in.shape[2]
    hb = sg_in.shape[2]
    half = hb // 2
    cw = half // NC
    tokens = tb * lax.axis_size("row")
    kick = float(tokens) ** (-0.5)
    v = pltpu.VMEM
    scratch = [
        v((tb, fb), BF),
        v((2, tokens, fb), BF),
        v((2, fb, tokens), BF),
        v((2, half, fb), BF),
        v((2, fb, half), BF),
        v((2, fb, half), BF),
        v((2, tb, half), BF),
        v((2, tb, half), BF),
        v((NC, 4, 2 * tb, cw), BF),
        v((NC, 3, 2 * tb, cw), BF),
        v((NC, 4, cw, 2 * tb), BF),
        v((NC, 4, 2 * tb, cw), BF),
        v((NC, 4, 2 * tb, cw), BF),
        v((NC, cw, fb), BF), v((NC, fb, cw), BF), v((NC, fb, cw), BF),
        v((NC, cw, fb), BF), v((NC, fb, cw), BF), v((NC, fb, cw), BF),
        v((fb, hb), F32), v((fb, hb), F32), v((hb, fb), F32),
        v((fb, hb), BF), v((fb, hb), BF), v((hb, fb), BF),
        v((fb, hb), BF), v((fb, hb), BF), v((hb, fb), BF),
        v((2, tokens, fb), F32),
        v((2, 2, 2 * tb, fb), BF),
        v((2, 2, 2 * tb, fb), BF),
        v((2, 4, tb, fb), BF),
        v((2, 4, tb, fb), BF),
        v((tb, fb), BF), v((tb, fb), BF), v((tb, fb), BF),
        pltpu.SemaphoreType.DMA((NSEM,)),
        pltpu.SemaphoreType.DMA((NSEM,)),
        pltpu.SemaphoreType.DMA((16,)),
        pltpu.SemaphoreType.DMA((2, NC, 6)),
    ]
    shape = jax.ShapeDtypeStruct
    outs = (
        shape(args[0].shape, BF),
        shape(args[4].shape, BF), shape(args[5].shape, BF), shape(args[6].shape, BF),
        shape(args[7].shape, F32), shape(args[8].shape, F32), shape(args[9].shape, F32),
    )
    work = 12 * tokens * fb * hb
    return pl.pallas_call(
        functools.partial(kernel, kick),
        out_shape=outs,
        in_specs=[pl.BlockSpec(memory_space=pl.ANY)] * 13,
        out_specs=[pl.BlockSpec(memory_space=pl.ANY)] * 7,
        scratch_shapes=scratch,
        compiler_params=pltpu.CompilerParams(
            collective_id=1, has_side_effects=True, vmem_limit_bytes=56 << 20
        ),
        cost_estimate=pl.CostEstimate(flops=work, bytes_accessed=12 << 20, transcendentals=0),
        name="relayed_step",
    )(*args)


def solution(mesh):
    feature = P("section", "col", "row")
    hidden = P("section", "row", "col")
    in_specs = (
        feature, feature, hidden, hidden, hidden, hidden, feature,
        hidden, hidden, feature, hidden, hidden, feature,
    )
    out_specs = (feature, hidden, hidden, feature, hidden, hidden, feature)
    return jax.shard_map(shards, mesh=mesh, in_specs=in_specs, out_specs=out_specs, check_vma=False)
```

time: 585 us -> 194 us (0.33)
  waiting for transfers between devices: 524 us -> 0 us
  Pallas kernels: 0 us -> 184 us
  matrix products: 24.1 us -> 0 us
  between operations: 14.3 us -> 0.65 us
    all_gather x5 -> x0, waiting for transfers between devices: 363 us -> none  [the longest x1 99.9 us: shards(): up_piece = lax.all_gather(up_grad, 'row', axis=0, tiled=True)]
    pallas_call x0 -> x1, Pallas kernels: none -> 184 us  [shards(): pl.pallas_call(functools.partial(kernel, kick), out_shape=outs, in_specs=...]
    reduce_scatter x2 -> x0, waiting for transfers between devices: 158 us -> none  [the longest x1 125 us: shards(): lax.psum_scatter(contract(grad_block, down_local, 1, 1).astype(jnp.bfloat...]
    dot_general x6 -> x0, matrix products: 24.1 us -> none  [contract(): lax.dot_general(left, right, (((left_dim,), (right_dim,)), ((), ())), pre...]
    unnamed x41 -> x17, local copies, waits for them, and re-layouts: 14.8 us -> 9.3 us
  transfers between devices with their start and end apart: 8 -> 0, of which waited for: 7 -> 0; matrix products, arithmetic and copies ran while one was open for 6% -> 0% of each run, Pallas kernels for 0% -> 0%
where the time goes in v1:
time: 194 us
  Pallas kernels  184 us (95%)
  local copies, waits for them, and re-layouts  9.3 us (5%)
    pallas_call x1, Pallas kernels, shards(): pl.pallas_call(functools.partial(kernel, kick), out_shape=outs, in_specs=...  184 us
    unnamed x17, local copies, waits for them, and re-layouts  9.3 us

profile of v1, /device:TPU:8, one launch (start us, length us, event | category | flops | bytes accessed | tf_op | source)
XLA Modules:
  0.0 193.7 jit_solution(14340053568385767137)
XLA Ops:
  0.6 183.8 %relayed_step.1 = (bf16[1,256,256]{2,1,0:T(8,128)(2,1)}, bf16[1,256,1024]{2,1,0:T(8,128)(2,1)}, bf16[1,256,1024]{2,1,0:T(8,128)(2,1)}, bf16[1,1024,256]{2,1,0:T(...) custom-call(bf16[1,256,256]{2,1,0:T(8,128)(2,1)} %x_in.1, ...), custom_call_target="tpu_custom_call" | custom-call | flops 6442450944 | bytes 12582912 | tf_op jit(solution)/shard_map/relayed_step/pallas_call | solution.py:465
  184.4 1.6 copy.27
  186.0 0.0 copy-start.4
  186.0 0.0 copy-start.3
  186.0 2.0 %copy.28 = bf16[1,256,1024]{2,1,0:T(8,128)(2,1)} copy(bf16[1,256,1024]{2,1,0:T(8,128)(2,1)} %get-tuple-element.15) | data formatting | bytes 1048576
  187.9 0.0 copy-done.4
  187.9 0.0 copy-start.2
  187.9 0.8 copy.29
  188.7 0.0 copy-done.3
  188.7 0.8 copy.30
  189.5 0.0 copy-done.2
  189.5 0.0 copy-start.1
  189.5 1.0 copy.31
  190.5 0.6 copy-done.1
  191.1 0.0 copy-start
  191.1 1.0 copy.32
  192.1 0.6 copy-done
  192.7 1.0 copy.33
Async XLA Ops:
  186.0 2.0 %copy-start.4 = (bf16[1,256,1024]{2,1,0:T(8,128)(2,1)S(1)}, bf16[1,256,1024]{2,1,0:T(8,128)(2,1)}, u32[]{:S(2)}) copy-start(bf16[1,256,1024]{2,1,0:T(8,128)(2,1)} %get-tuple-element.16) | copy-start | bytes 1572868
  186.0 2.8 %copy-start.3 = (bf16[1,1024,256]{2,1,0:T(8,128)(2,1)S(1)}, bf16[1,1024,256]{2,1,0:T(8,128)(2,1)}, u32[]{:S(2)}) copy-start(bf16[1,1024,256]{2,1,0:T(8,128)(2,1)} %get-tuple-element.17) | copy-start | bytes 1572868
  187.9 1.6 copy-start.2
  189.5 1.6 copy-start.1
  191.1 1.6 copy-start

commit v2 on v1

v2 whole, which is shorter than its diff:
```python
import functools

import jax
import jax.numpy as jnp
from jax import lax
from jax.experimental import pallas as pl
from jax.experimental.pallas import tpu as pltpu
from jax.sharding import PartitionSpec as P

FRICTION = 0.1
DRIFT = 0.01
MESH = pl.DeviceIdType.MESH
BF = jnp.bfloat16
F32 = jnp.float32
NC = 4
DN_FIRST = 4
SG_FIRST = 4
HG_FIRST = 2
X_FIRST = True
X_BESIDE = {1: (), 2: (), 3: (0,), 4: ()}
LAG = 3
X_AFTER = ()
X_TURNS = ((1, 0), (2, 1), (3, 2), (4, 3))

DN, SGX, SUX, GTX, UPX = 0, NC, 2 * NC, 3 * NC, 4 * NC
DYR = 5 * NC
DYC = DYR + 14
XR = DYC + 8
XC = XR + 14
RS = XC + 8
AG = RS + 3 * NC
AF = AG + 4 * NC
WX = AF + 4 * NC
HA = WX + 3 * NC
HF = HA + 2 * NC
DXC = HF + 2 * NC
DXR = DXC + 4
FIN = DXR + 16
NSEM = FIN + 2


def nt(a, b):
    return lax.dot_general(a, b, (((1,), (1,)), ((), ())), preferred_element_type=F32)


def nn(a, b):
    return jnp.dot(a, b, preferred_element_type=F32)


def kernel(
    x_in, dy_in, sg_in, su_in, wg_in, wu_in, wd_in,
    prev_out, gg_out, gu_out, gd_out,
    x_stage, dyf, xt, down_f, gate_f, up_f, sg_f, su_f, hgs, rsr, ht, g, u,
    wds, wgs, wus, owd, owg, owu, acc, dxs, dxr, psend, precv, fin,
    ssem, rsem, lsem, osem,
):
    tb, fb = x_in.shape[1], x_in.shape[2]
    half = sg_in.shape[2] // 2
    cw = half // NC
    xb = 2 * tb

    y, row, col = lax.axis_index("section"), lax.axis_index("row"), lax.axis_index("col")
    zh, x, zl, core = row // 4, row % 4, col // 2, col % 2
    z = zh * 4 + zl
    oh = 1 - zh

    def at_z(zz):
        return (y, (zz // 4) * 4 + x, (zz % 4) * 2 + core)

    def at_x(xx):
        return (y, zh * 4 + xx, col)

    partner = (y, oh * 4 + x, col)
    z_next, z_prev = at_z((z + 1) % 8), at_z((z + 7) % 8)
    x1, x2, x3 = (x + 1) % 4, (x + 2) % 4, (x + 3) % 4
    x_next, x_prev, x_far = at_x(x1), at_x(x3), at_x(x2)
    twin = (y, row, zl * 2 + 1 - core)
    y_prev, y_next = ((y + 3) % 4, row, col), ((y + 1) % 4, row, col)

    def rcopy(src, dst, sem, to):
        return pltpu.make_async_remote_copy(
            src_ref=src, dst_ref=dst, send_sem=ssem.at[sem], recv_sem=rsem.at[sem],
            device_id=to, device_id_type=MESH,
        )

    def send(src, dst, sem, to):
        rcopy(src, dst, sem, to).start()

    def got(dst, sem):
        rcopy(dst, dst, sem, partner).wait_recv()

    def sent(src, sem):
        rcopy(src, src, sem, partner).wait_send()

    def cols(at, j):
        return pl.ds(pl.multiple_of(at * half + j * cw, cw), cw)

    def chunk(j):
        return pl.ds(pl.multiple_of(j * cw, cw), cw)

    def place(zz, kk):
        return ((((zz % 2) * 2 + kk) * 2) + (zz % 4) // 2) * tb

    def dy_slot(zz, kk, first=0, size=tb):
        return dyf.at[zz // 4, pl.ds(pl.multiple_of(place(zz, kk) + first, 16), size)]

    def x_slot(zz, kk, first=0, size=fb):
        return xt.at[zz // 4, pl.ds(first, size), pl.ds(pl.multiple_of(place(zz, kk), tb), tb)]

    bar = pltpu.get_barrier_semaphore()
    for to in (partner, z_next, z_prev, x_next, x_prev, x_far, twin, y_next):
        pl.semaphore_signal(bar, inc=1, device_id=to, device_id_type=MESH)

    own_half = pl.ds(pl.multiple_of(zh * half, half), half)
    loads = [
        pltpu.make_async_copy(s, d, lsem.at[i])
        for i, (s, d) in enumerate([
            (x_in.at[0], x_stage),
            (dy_in.at[0], dy_slot(z, core)),
            (wd_in.at[0, own_half], down_f.at[zh]),
            (sg_in.at[0, :, own_half], sg_f.at[zh]),
            (su_in.at[0, :, own_half], su_f.at[zh]),
            (wg_in.at[0, :, own_half], gate_f.at[zh]),
            (wu_in.at[0, :, own_half], up_f.at[zh]),
        ])
    ]
    for load in loads:
        load.start()
    pl.semaphore_wait(bar, 8)

    def pieces(slot):
        size = (tb if slot is dy_slot else fb) // 2
        return (0, size), (size, size)

    def ring_sem(base, step, d, p):
        return base + (4 * step + 2 * d + p if step < 3 else 12 + d)

    def ring(slot, base, cbase, step):
        back, ahead = (z + 8 - step) % 8, (z + step) % 8
        for p, cut in enumerate(pieces(slot)):
            for d, (block, to) in enumerate(((back, z_next), (ahead, z_prev))):
                if 1 <= step <= 3 or (step == 4 and d == p):
                    got(slot(block, core, *cut), ring_sem(base, step - 1, d, p))
                if step < 3 or (step == 3 and d == p):
                    send(slot(block, core, *cut), slot(block, core, *cut), ring_sem(base, step, d, p), to)
        if step == 0 or step == 4:
            send(slot(back, core), slot(back, core), cbase + (7 if step else 0), twin)
        else:
            send(slot(back, core), slot(back, core), cbase + 2 * step - 1, twin)
            send(slot(ahead, core), slot(ahead, core), cbase + 2 * step, twin)

    def ring_order():
        return [(0, z)] + [
            (2 * s - 1 + d, (z + 8 - s) % 8 if d == 0 else (z + s) % 8) for s in (1, 2, 3) for d in (0, 1)
        ] + [(7, (z + 4) % 8)]

    def ring_sent(slot, base, cbase):
        for i in range(14):
            sent(slot(z, core, *pieces(slot)[0]), base + i)
        for i in range(8):
            sent(slot(z, core), cbase + i)

    def send_down(j):
        there = pl.ds(pl.multiple_of(oh * half + j * cw, cw), cw)
        send(wd_in.at[0, there], down_f.at[zh, chunk(j)], DN + j, partner)

    def send_saved(j):
        send(sg_in.at[0, :, cols(oh, j)], sg_f.at[zh, :, chunk(j)], SGX + j, partner)
        send(su_in.at[0, :, cols(oh, j)], su_f.at[zh, :, chunk(j)], SUX + j, partner)

    loads[1].wait()
    ring(dy_slot, DYR, DYC, 0)

    pl.loop(0, DN_FIRST)(send_down)

    loads[0].wait()
    x_slot_own = x_slot(z, core)
    x_slot_own[...] = x_stage[...].astype(F32).T.astype(BF)
    acc[...] = jnp.zeros_like(acc)

    for step in (1, 2, 3):
        ring(dy_slot, DYR, DYC, step)
        for x_step in X_BESIDE[step]:
            ring(x_slot, XR, XC, x_step)
    if DN_FIRST < NC:
        pl.loop(DN_FIRST, NC)(send_down)
    pl.loop(0, SG_FIRST)(send_saved)
    ring(dy_slot, DYR, DYC, 4)
    for x_step in X_BESIDE[4]:
        ring(x_slot, XR, XC, x_step)
    loads[2].wait()
    for i, zz in ring_order():
        got(dy_slot(zz, 1 - core), DYC + i)

    def partial_hidden(j):
        got(down_f.at[oh, chunk(j)], DN + j)

        @pl.loop(0, 4)
        def _(xx):
            rows = pl.ds(pl.multiple_of(xx * xb, xb), xb)
            hgs[j, xx] = (
                nt(dyf[0, rows, :], down_f[0, chunk(j), :]) + nt(dyf[1, rows, :], down_f[1, chunk(j), :])
            ).astype(BF)

        send(hgs.at[j, x1], rsr.at[j, 0], RS + 3 * j, x_next)
        send(hgs.at[j, x2], rsr.at[j, 1], RS + 3 * j + 1, x_far)
        send(hgs.at[j, x3], rsr.at[j, 2], RS + 3 * j + 2, x_prev)

    pl.loop(0, HG_FIRST)(partial_hidden)
    for x_step in X_AFTER:
        ring(x_slot, XR, XC, x_step)
    if SG_FIRST < NC:
        pl.loop(SG_FIRST, NC)(send_saved)
    for i in (3, 4, 5, 6):
        loads[i].wait()

    def send_weights(j):
        send(wg_in.at[0, :, cols(oh, j)], gate_f.at[zh, :, chunk(j)], GTX + j, partner)
        send(wu_in.at[0, :, cols(oh, j)], up_f.at[zh, :, chunk(j)], UPX + j, partner)

    def activations(j):
        for d in range(3):
            got(rsr.at[j, d], RS + 3 * j + d)
        got(sg_f.at[oh, :, chunk(j)], SGX + j)
        got(su_f.at[oh, :, chunk(j)], SUX + j)
        for part in range(2):
            rows = pl.ds(part * tb, tb)
            hidden_grad = hgs[j, x, rows, :].astype(F32)
            for d in range(3):
                hidden_grad = hidden_grad + rsr[j, d, rows, :].astype(F32)
            gate_pre = sg_f[part, :, chunk(j)].astype(F32)
            up_pre = su_f[part, :, chunk(j)].astype(F32)
            sigmoid_gate = jax.nn.sigmoid(gate_pre)
            silu_gate = gate_pre * sigmoid_gate
            slope = sigmoid_gate * (1.0 + gate_pre * (1.0 - sigmoid_gate))
            g[j, x, rows, :] = (hidden_grad * up_pre * slope).astype(BF)
            u[j, x, rows, :] = (hidden_grad * silu_gate).astype(BF)
            ht[j, x, :, rows] = (silu_gate * up_pre).T.astype(BF)
        for i, ref in enumerate((g, u)):
            send(ref.at[j, x], ref.at[j, x], AG + 4 * j + i, x_next)
            send(ref.at[j, x], ref.at[j, x], AG + 4 * j + 2 + i, x_prev)

    def send_hidden(j):
        send(ht.at[j, x], ht.at[j, x], HA + 2 * j, x_next)
        send(ht.at[j, x], ht.at[j, x], HA + 2 * j + 1, x_prev)

    def halves(ref, j, xx, second):
        size = ref.shape[2] // 2
        return ref.at[j, xx, pl.ds(second * size, size)]

    def pass_on(ref, j, base, far):
        got(ref.at[j, x3], base)
        send(halves(ref, j, x3, 0), halves(ref, j, x3, 0), far, x_next)

    def pass_back(ref, j, base, far):
        got(ref.at[j, x1], base)
        send(halves(ref, j, x1, 1), halves(ref, j, x1, 1), far, x_prev)

    def forward(j):
        for i, ref in enumerate((g, u)):
            pass_on(ref, j, AG + 4 * j + i, AF + 4 * j + i)
            pass_back(ref, j, AG + 4 * j + 2 + i, AF + 4 * j + 2 + i)

    def forward_hidden(j):
        pass_on(ht, j, HA + 2 * j, HF + 2 * j)
        pass_back(ht, j, HA + 2 * j + 1, HF + 2 * j + 1)

    def down_grad(j, at):
        total = nn(ht[j, 0], dyf[at, pl.ds(0, xb), :])
        for xx in range(1, 4):
            total = total + nn(ht[j, xx], dyf[at, pl.ds(xx * xb, xb), :])
        return total.astype(BF)

    def column_grad(j, at, ref):
        total = nn(xt[at, :, pl.ds(0, xb)], ref[j, 0])
        for xx in range(1, 4):
            total = total + nn(xt[at, :, pl.ds(xx * xb, xb)], ref[j, xx])
        return total.astype(BF)

    def keep(i, own, out, where, j):
        pltpu.make_async_copy(own.at[j], out.at[where], osem.at[j, i]).start()

    def column_grads(j):
        for i, ref in enumerate((g, u)):
            got(halves(ref, j, x2, 0), AF + 4 * j + i)
            got(halves(ref, j, x2, 1), AF + 4 * j + 2 + i)
        got(gate_f.at[oh, :, chunk(j)], GTX + j)
        got(up_f.at[oh, :, chunk(j)], UPX + j)

        @pl.loop(0, 4)
        def _(xx):
            rows = pl.ds(pl.multiple_of(xx * xb, xb), xb)
            for at in range(2):
                acc[at, rows, :] += nt(g[j, xx], gate_f[at, :, chunk(j)]) + nt(u[j, xx], up_f[at, :, chunk(j)])

        @pl.when(j == NC - 1)
        def _():
            for m in range(2):
                for at in range(2):
                    rows = pl.ds(pl.multiple_of((1 - core + 2 * m) * xb, xb), xb)
                    dxs[at, m] = acc[at, rows, :].astype(BF)
                    send(dxs.at[at, m], dxr.at[at, m], DXC + 2 * m + at, twin)

        for i, (ref, theirs, own, out) in enumerate(((g, wgs, owg, gg_out), (u, wus, owu, gu_out))):
            theirs[j] = column_grad(j, oh, ref)
            send(theirs.at[j], out.at[:, cols(zh, j)], WX + 3 * j + 1 + i, partner)

        for i, (ref, own, out) in enumerate(((g, owg, gg_out), (u, owu, gu_out))):
            own[j] = column_grad(j, zh, ref)
            keep(1 + i, own, out, (slice(None), cols(zh, j)), j)

    def row_grads(j):
        got(halves(ht, j, x2, 0), HF + 2 * j)
        got(halves(ht, j, x2, 1), HF + 2 * j + 1)
        wds[j] = down_grad(j, oh)
        send(wds.at[j], gd_out.at[cols(zh, j), :], WX + 3 * j, partner)
        owd[j] = down_grad(j, zh)
        keep(0, owd, gd_out, (cols(zh, j),), j)

    @pl.loop(0, NC + LAG)
    def _(i):
        @pl.when(i < NC)
        def _():
            activations(i)

        if HG_FIRST < NC:
            @pl.when(i < NC - HG_FIRST)
            def _():
                partial_hidden(i + HG_FIRST)

        for step, turn in X_TURNS:
            @pl.when(i == turn)
            def _():
                ring(x_slot, XR, XC, step)
                if step == 4:
                    for n, zz in ring_order():
                        got(x_slot(zz, 1 - core), XC + n)

        for turn, first in ((1, 0), (2, 2)):
            @pl.when(i == turn)
            def _():
                send_weights(first)
                send_weights(first + 1)

        @pl.when((i >= 1) & (i <= NC))
        def _():
            forward(i - 1)

        @pl.when(i == NC)
        def _():
            pl.loop(0, NC)(send_hidden)

        @pl.when(i >= LAG)
        def _():
            column_grads(i - LAG)

    pl.loop(0, NC)(forward_hidden)
    for m in range(2):
        for at in range(2):
            got(dxr.at[at, m], DXC + 2 * m + at)

    def part(zz, first=0, size=tb):
        at, late, m = zz // 4, (zz % 4) // 2, zz % 2
        mine = pl.ds(pl.multiple_of(((core + 2 * m) * 2 + late) * tb + first, 16), size)
        other = pl.ds(pl.multiple_of(late * tb + first, 16), size)
        return acc[at, mine, :] + dxr[at, m, other, :].astype(F32)

    ht2 = tb // 2

    def dx_sem(step, d, p):
        return DXR + 4 * step + 2 * d + p

    for step in range(4):
        for p in range(2):
            rows = pl.ds(p * ht2, ht2)
            for d in range(2):
                to = (z + 4 - step) % 8 if d == 0 else (z + 4 + step) % 8
                if step == 0 and p != d:
                    continue
                total = part(to, p * ht2, ht2)
                if step >= 2 or (step == 1 and p == d):
                    got(precv.at[d, step - 1, rows], dx_sem(step - 1, d, p))
                    total = total + precv[d, step - 1, rows, :].astype(F32)
                psend[d, step, rows, :] = total.astype(BF)
                send(psend.at[d, step, rows], precv.at[d, step, rows], dx_sem(step, d, p), z_next if d == 0 else z_prev)
        if step >= 1:
            row_grads(step - 1)

    for p in range(2):
        rows = pl.ds(p * ht2, ht2)
        total = part(z, p * ht2, ht2)
        for d in range(2):
            got(precv.at[d, 3, rows], dx_sem(3, d, p))
            total = total + precv[d, 3, rows, :].astype(F32)
        fin[rows, :] = total.astype(BF)
        send(fin.at[rows], prev_out.at[rows], FIN + p, y_prev)
    row_grads(NC - 1)
    for p in range(2):
        got(prev_out.at[pl.ds(p * ht2, ht2)], FIN + p)

    ring_sent(dy_slot, DYR, DYC)
    ring_sent(x_slot, XR, XC)

    @pl.loop(0, NC)
    def _(j):
        sent(down_f.at[0, chunk(j)], DN + j)
        for ref, base in ((sg_f, SGX), (su_f, SUX), (gate_f, GTX), (up_f, UPX)):
            sent(ref.at[0, :, chunk(j)], base + j)
        for d in range(3):
            sent(rsr.at[j, d], RS + 3 * j + d)
        for i, ref in enumerate((g, u)):
            for d in range(2):
                sent(ref.at[j, 0], AG + 4 * j + 2 * d + i)
                sent(halves(ref, j, 0, 0), AF + 4 * j + 2 * d + i)
        for d in range(2):
            sent(ht.at[j, 0], HA + 2 * j + d)
            sent(halves(ht, j, 0, 0), HF + 2 * j + d)
        mine = (gd_out.at[cols(zh, j), :], gg_out.at[:, cols(zh, j)], gu_out.at[:, cols(zh, j)])
        theirs = (gd_out.at[cols(oh, j), :], gg_out.at[:, cols(oh, j)], gu_out.at[:, cols(oh, j)])
        for i, (ref, own, out, arrived) in enumerate(zip((wds, wgs, wus), (owd, owg, owu), mine, theirs)):
            sent(ref.at[j], WX + 3 * j + i)
            pltpu.make_async_copy(own.at[j], out, osem.at[j, i]).wait()
            got(arrived, WX + 3 * j + i)

    for i in range(4):
        sent(dxs.at[0, 0], DXC + i)
    for step in range(4):
        for d in range(2):
            for p in range(2):
                if step > 0 or p == d:
                    sent(psend.at[d, step, pl.ds(0, ht2)], dx_sem(step, d, p))
    for p in range(2):
        sent(fin.at[pl.ds(0, ht2)], FIN + p)


def update(kick, w_ref, m_ref, n_ref, grad_ref, w_out, m_out):
    moved = (
        (1.0 - FRICTION) * m_ref[0]
        - kick * grad_ref[...].astype(F32)
        + (2.0 * FRICTION) ** 0.5 * n_ref[0].astype(F32)
    )
    m_out[0] = moved
    w_out[0] = (w_ref[0].astype(F32) + DRIFT * moved).astype(BF)


def update_all(kick, prev, gg, gu, gd, mg, mu, md, ng, nu, nd, wg, wu, wd, *outs):
    prev_out, wg_out, wu_out, wd_out, mg_out, mu_out, md_out = outs
    last = lax.axis_index("section") == lax.axis_size("section") - 1
    prev_out[0] = jnp.where(last, jnp.zeros_like(prev), prev[...])
    update(kick, wg, mg, ng, gg, wg_out, mg_out)
    update(kick, wu, mu, nu, gu, wu_out, mu_out)
    update(kick, wd, md, nd, gd, wd_out, md_out)


def shards(*args):
    x_in, sg_in = args[0], args[2]
    tb, fb = x_in.shape[1], x_in.shape[2]
    hb = sg_in.shape[2]
    half = hb // 2
    cw = half // NC
    tokens = tb * lax.axis_size("row")
    kick = float(tokens) ** (-0.5)
    v = pltpu.VMEM
    scratch = [
        v((tb, fb), BF),
        v((2, tokens, fb), BF),
        v((2, fb, tokens), BF),
        v((2, half, fb), BF),
        v((2, fb, half), BF),
        v((2, fb, half), BF),
        v((2, tb, half), BF),
        v((2, tb, half), BF),
        v((NC, 4, 2 * tb, cw), BF),
        v((NC, 3, 2 * tb, cw), BF),
        v((NC, 4, cw, 2 * tb), BF),
        v((NC, 4, 2 * tb, cw), BF),
        v((NC, 4, 2 * tb, cw), BF),
        v((NC, cw, fb), BF), v((NC, fb, cw), BF), v((NC, fb, cw), BF),
        v((NC, cw, fb), BF), v((NC, fb, cw), BF), v((NC, fb, cw), BF),
        v((2, tokens, fb), F32),
        v((2, 2, 2 * tb, fb), BF),
        v((2, 2, 2 * tb, fb), BF),
        v((2, 4, tb, fb), BF),
        v((2, 4, tb, fb), BF),
        v((tb, fb), BF),
        pltpu.SemaphoreType.DMA((NSEM,)),
        pltpu.SemaphoreType.DMA((NSEM,)),
        pltpu.SemaphoreType.DMA((7,)),
        pltpu.SemaphoreType.DMA((NC, 3)),
    ]
    shape = jax.ShapeDtypeStruct
    work = 12 * tokens * fb * hb
    prev, gg, gu, gd = pl.pallas_call(
        kernel,
        out_shape=(shape((tb, fb), BF), shape((fb, hb), BF), shape((fb, hb), BF), shape((hb, fb), BF)),
        in_specs=[pl.BlockSpec(memory_space=pltpu.HBM)] * 7,
        out_specs=[pl.BlockSpec(memory_space=pl.ANY)] * 4,
        scratch_shapes=scratch,
        compiler_params=pltpu.CompilerParams(
            collective_id=1, has_side_effects=True, vmem_limit_bytes=52 << 20
        ),
        cost_estimate=pl.CostEstimate(flops=work, bytes_accessed=12 << 20, transcendentals=0),
        name="relayed_gradients",
    )(*args[:7])

    steps = 4
    thin, wide = pl.BlockSpec((fb // steps, hb), lambda i: (i, 0)), pl.BlockSpec((1, fb // steps, hb), lambda i: (0, i, 0))
    low, tall = pl.BlockSpec((hb // steps, fb), lambda i: (i, 0)), pl.BlockSpec((1, hb // steps, fb), lambda i: (0, i, 0))
    block, block_out = pl.BlockSpec((tb // steps, fb), lambda i: (i, 0)), pl.BlockSpec((1, tb // steps, fb), lambda i: (0, i, 0))
    outs = (
        shape(args[0].shape, BF),
        shape(args[4].shape, BF), shape(args[5].shape, BF), shape(args[6].shape, BF),
        shape(args[7].shape, F32), shape(args[8].shape, F32), shape(args[9].shape, F32),
    )
    return pl.pallas_call(
        functools.partial(update_all, kick),
        grid=(steps,),
        out_shape=outs,
        in_specs=[block, thin, thin, low] + [wide, wide, tall] * 3,
        out_specs=[block_out] + [wide, wide, tall] * 2,
        compiler_params=pltpu.CompilerParams(vmem_limit_bytes=16 << 20),
        name="sghmc_update",
    )(prev, gg, gu, gd, *args[7:10], *args[10:13], *args[4:7])


def solution(mesh):
    feature = P("section", "col", "row")
    hidden = P("section", "row", "col")
    in_specs = (
        feature, feature, hidden, hidden, hidden, hidden, feature,
        hidden, hidden, feature, hidden, hidden, feature,
    )
    out_specs = (feature, hidden, hidden, feature, hidden, hidden, feature)
    return jax.shard_map(shards, mesh=mesh, in_specs=in_specs, out_specs=out_specs, check_vma=False)
```

time: 194 us -> 153 us (0.79)
  Pallas kernels: 184 us -> 149 us
  local copies, waits for them, and re-layouts: 9.3 us -> 2.56 us
    pallas_call x1 -> x2, Pallas kernels: 184 us -> 149 us  [the longest x1 146 us: shards(): pl.pallas_call(kernel, out_shape=(shape((tb, fb), BF), shape((fb, hb), BF...]
    unnamed x17 -> x22, local copies, waits for them, and re-layouts: 9.3 us -> 2.56 us
where the time goes in v2:
time: 153 us
  Pallas kernels  149 us (97%)
  local copies, waits for them, and re-layouts  2.56 us (2%)
    pallas_call x1, Pallas kernels, shards(): pl.pallas_call(kernel, out_shape=(shape((tb, fb), BF), shape((fb, hb), BF...  146 us

profile of v2, /device:TPU:8, one launch (start us, length us, event | category | flops | bytes accessed | tf_op | source)
XLA Modules:
  0.0 152.7 jit_solution(4731230667120322438)
XLA Ops:
  0.6 0.0 copy-start.5
  0.6 0.0 copy-start.4
  0.7 0.0 copy-start.3
  0.7 0.0 copy-start.8
  0.7 0.0 copy-start.7
  0.7 0.0 copy-start.6
  0.7 0.0 copy-start.2
  0.7 0.0 copy-start.1
  0.7 0.0 copy-start
  0.7 0.0 copy-start.9
  0.7 1.0 copy-done.9
  1.8 0.0 copy-start.10
  1.8 1.5 copy-done.10
  3.3 146.4 %relayed_gradients.1 = (bf16[256,256]{1,0:T(8,128)(2,1)S(1)}, bf16[256,1024]{1,0:T(8,128)(2,1)S(1)}, bf16[256,1024]{1,0:T(8,128)(2,1)S(1)}, bf16[1024,256]{1,0:T(8,128)(2,1)S(1)}) custom-call(bf16[1,256,256]{2,1,0:T(8,128)(2,1)S(1)} %copy-done.9, bf16[1,256,256]{2,1,0:T(8,128)(2,1)S(1)} %copy-done.10, bf16[1,256,1024]{2,1,0:T(8,128)(2,1)} %sg_in.1, ...), custom_call_target="tpu_custom_call" | custom-call | flops 6442450944 | bytes 12582912 | tf_op jit(solution)/shard_map/relayed_gradients/pallas_call | solution.py:493
  149.7 0.0 copy-done.5
  149.7 0.0 copy-done.4
  149.7 0.0 copy-done.3
  149.7 0.0 copy-done.8
  149.7 0.0 copy-done.7
  149.8 0.0 copy-done.6
  149.8 0.0 copy-done.2
  149.8 0.0 copy-done.1
  149.8 0.0 copy-done
  149.8 2.9 %sghmc_update.1 = (bf16[1,256,256]{2,1,0:T(8,128)(2,1)}, bf16[1,256,1024]{2,1,0:T(8,128)(2,1)}, bf16[1,256,1024]{2,1,0:T(8,128)(2,1)}, bf16[1,1024,256]{2,1,0:T(...) custom-call(bf16[256,256]{1,0:T(8,128)(2,1)S(1)} %get-tuple-element.11.prev, ...), custom_call_target="tpu_custom_call" | custom-call | tf_op jit(solution)/shard_map/sghmc_update/pallas_call | solution.py:515
Async XLA Ops:
  0.6 149.1 %copy-start.5 = (bf16[1,1024,256]{2,1,0:T(8,128)(2,1)S(1)}, bf16[1,1024,256]{2,1,0:T(8,128)(2,1)}, u32[]{:S(2)}) copy-start(bf16[1,1024,256]{2,1,0:T(8,128)(2,1)} %wd.1) | copy-start | bytes 1572868
  0.6 149.1 %copy-start.4 = (bf16[1,256,1024]{2,1,0:T(8,128)(2,1)S(1)}, bf16[1,256,1024]{2,1,0:T(8,128)(2,1)}, u32[]{:S(2)}) copy-start(bf16[1,256,1024]{2,1,0:T(8,128)(2,1)} %wu.1) | copy-start | bytes 1572868
  0.7 149.1 %copy-start.3 = (bf16[1,256,1024]{2,1,0:T(8,128)(2,1)S(1)}, bf16[1,256,1024]{2,1,0:T(8,128)(2,1)}, u32[]{:S(2)}) copy-start(bf16[1,256,1024]{2,1,0:T(8,128)(2,1)} %wg.1) | copy-start | bytes 1572868
  0.7 149.1 %copy-start.8 = (bf16[1,1024,256]{2,1,0:T(8,128)(2,1)S(1)}, bf16[1,1024,256]{2,1,0:T(8,128)(2,1)}, u32[]{:S(2)}) copy-start(bf16[1,1024,256]{2,1,0:T(8,128)(2,1)} %nd.1) | copy-start | bytes 1572868
  0.7 149.1 %copy-start.7 = (bf16[1,256,1024]{2,1,0:T(8,128)(2,1)S(1)}, bf16[1,256,1024]{2,1,0:T(8,128)(2,1)}, u32[]{:S(2)}) copy-start(bf16[1,256,1024]{2,1,0:T(8,128)(2,1)} %nu.1) | copy-start | bytes 1572868
  0.7 149.1 %copy-start.6 = (bf16[1,256,1024]{2,1,0:T(8,128)(2,1)S(1)}, bf16[1,256,1024]{2,1,0:T(8,128)(2,1)}, u32[]{:S(2)}) copy-start(bf16[1,256,1024]{2,1,0:T(8,128)(2,1)} %ng.1) | copy-start | bytes 1572868
  0.7 149.1 %copy-start.2 = (f32[1,1024,256]{2,1,0:T(8,128)S(1)}, f32[1,1024,256]{2,1,0:T(8,128)}, u32[]{:S(2)}) copy-start(f32[1,1024,256]{2,1,0:T(8,128)} %md.1) | copy-start | bytes 3145732
  0.7 149.1 %copy-start.1 = (f32[1,256,1024]{2,1,0:T(8,128)S(1)}, f32[1,256,1024]{2,1,0:T(8,128)}, u32[]{:S(2)}) copy-start(f32[1,256,1024]{2,1,0:T(8,128)} %mu.1) | copy-start | bytes 3145732
  0.7 149.1 %copy-start = (f32[1,256,1024]{2,1,0:T(8,128)S(1)}, f32[1,256,1024]{2,1,0:T(8,128)}, u32[]{:S(2)}) copy-start(f32[1,256,1024]{2,1,0:T(8,128)} %mg.1) | copy-start | bytes 3145732
  0.7 1.1 copy-start.9
  1.8 1.5 copy-start.10

commit v3 on v2

--- a/solution.py
+++ b/solution.py
@@ -14,7 +14,7 @@
 F32 = jnp.float32
 NC = 4
 DN_FIRST = 4
-SG_FIRST = 4
+SG_FIRST = 2
 HG_FIRST = 2
 X_FIRST = True
 X_BESIDE = {1: (), 2: (), 3: (0,), 4: ()}
@@ -36,7 +36,8 @@
 DXC = HF + 2 * NC
 DXR = DXC + 4
 FIN = DXR + 16
-NSEM = FIN + 2
+HE = FIN + 2
+NSEM = HE + 4
 
 
 def nt(a, b):
@@ -176,6 +177,30 @@
     loads[0].wait()
     x_slot_own = x_slot(z, core)
     x_slot_own[...] = x_stage[...].astype(F32).T.astype(BF)
+
+    def token_columns(part):
+        return pl.ds(pl.multiple_of(part * tb, tb), tb)
+
+    def cut_rows(second):
+        return pl.ds(0, cw) if second is None else pl.ds(second * (cw // 2), cw // 2)
+
+    def early(xx, second=None):
+        return ht.at[:, xx, cut_rows(second), token_columns(zh)]
+
+    def late(j, xx, second=None):
+        return ht.at[j, xx, cut_rows(second), token_columns(oh)]
+
+    def hidden_value(part, j):
+        gate_pre = sg_f[part, :, chunk(j)].astype(F32)
+        up_pre = su_f[part, :, chunk(j)].astype(F32)
+        value = gate_pre * jax.nn.sigmoid(gate_pre) * up_pre
+        ht[j, x, :, token_columns(part)] = value.T.astype(BF)
+
+    loads[3].wait()
+    loads[4].wait()
+    pl.loop(0, NC)(functools.partial(hidden_value, zh))
+    send(early(x), early(x), HE, x_next)
+    send(early(x), early(x), HE + 1, x_prev)
     acc[...] = jnp.zeros_like(acc)
 
     for step in (1, 2, 3):
@@ -186,6 +211,10 @@
         pl.loop(DN_FIRST, NC)(send_down)
     pl.loop(0, SG_FIRST)(send_saved)
     ring(dy_slot, DYR, DYC, 4)
+    got(early(x3), HE)
+    send(early(x3, 0), early(x3, 0), HE + 2, x_next)
+    got(early(x1), HE + 1)
+    send(early(x1, 1), early(x1, 1), HE + 3, x_prev)
     for x_step in X_BESIDE[4]:
         ring(x_slot, XR, XC, x_step)
     loads[2].wait()
@@ -211,7 +240,7 @@
         ring(x_slot, XR, XC, x_step)
     if SG_FIRST < NC:
         pl.loop(SG_FIRST, NC)(send_saved)
-    for i in (3, 4, 5, 6):
+    for i in (5, 6):
         loads[i].wait()
 
     def send_weights(j):
@@ -223,6 +252,7 @@
             got(rsr.at[j, d], RS + 3 * j + d)
         got(sg_f.at[oh, :, chunk(j)], SGX + j)
         got(su_f.at[oh, :, chunk(j)], SUX + j)
+        hidden_value(oh, j)
         for part in range(2):
             rows = pl.ds(part * tb, tb)
             hidden_grad = hgs[j, x, rows, :].astype(F32)
@@ -231,18 +261,16 @@
             gate_pre = sg_f[part, :, chunk(j)].astype(F32)
             up_pre = su_f[part, :, chunk(j)].astype(F32)
             sigmoid_gate = jax.nn.sigmoid(gate_pre)
-            silu_gate = gate_pre * sigmoid_gate
             slope = sigmoid_gate * (1.0 + gate_pre * (1.0 - sigmoid_gate))
             g[j, x, rows, :] = (hidden_grad * up_pre * slope).astype(BF)
-            u[j, x, rows, :] = (hidden_grad * silu_gate).astype(BF)
-            ht[j, x, :, rows] = (silu_gate * up_pre).T.astype(BF)
+            u[j, x, rows, :] = (hidden_grad * (gate_pre * sigmoid_gate)).astype(BF)
         for i, ref in enumerate((g, u)):
             send(ref.at[j, x], ref.at[j, x], AG + 4 * j + i, x_next)
             send(ref.at[j, x], ref.at[j, x], AG + 4 * j + 2 + i, x_prev)
 
     def send_hidden(j):
-        send(ht.at[j, x], ht.at[j, x], HA + 2 * j, x_next)
-        send(ht.at[j, x], ht.at[j, x], HA + 2 * j + 1, x_prev)
+        send(late(j, x), late(j, x), HA + 2 * j, x_next)
+        send(late(j, x), late(j, x), HA + 2 * j + 1, x_prev)
 
     def halves(ref, j, xx, second):
         size = ref.shape[2] // 2
@@ -262,8 +290,10 @@
             pass_back(ref, j, AG + 4 * j + 2 + i, AF + 4 * j + 2 + i)
 
     def forward_hidden(j):
-        pass_on(ht, j, HA + 2 * j, HF + 2 * j)
-        pass_back(ht, j, HA + 2 * j + 1, HF + 2 * j + 1)
+        got(late(j, x3), HA + 2 * j)
+        send(late(j, x3, 0), late(j, x3, 0), HF + 2 * j, x_next)
+        got(late(j, x1), HA + 2 * j + 1)
+        send(late(j, x1, 1), late(j, x1, 1), HF + 2 * j + 1, x_prev)
 
     def down_grad(j, at):
         total = nn(ht[j, 0], dyf[at, pl.ds(0, xb), :])
@@ -280,10 +310,23 @@
     def keep(i, own, out, where, j):
         pltpu.make_async_copy(own.at[j], out.at[where], osem.at[j, i]).start()
 
-    def column_grads(j):
+    def partner_columns(j):
         for i, ref in enumerate((g, u)):
             got(halves(ref, j, x2, 0), AF + 4 * j + i)
             got(halves(ref, j, x2, 1), AF + 4 * j + 2 + i)
+        send_columns(j)
+
+    def send_columns(j):
+        for i, (ref, theirs, out) in enumerate(((g, wgs, gg_out), (u, wus, gu_out))):
+            theirs[j] = column_grad(j, oh, ref)
+            send(theirs.at[j], out.at[:, cols(zh, j)], WX + 3 * j + 1 + i, partner)
+
+    def own_columns(j):
+        for i, (ref, own, out) in enumerate(((g, owg, gg_out), (u, owu, gu_out))):
+            own[j] = column_grad(j, zh, ref)
+            keep(1 + i, own, out, (slice(None), cols(zh, j)), j)
+
+    def add_input_grad(j):
         got(gate_f.at[oh, :, chunk(j)], GTX + j)
         got(up_f.at[oh, :, chunk(j)], UPX + j)
 
@@ -293,31 +336,15 @@
             for at in range(2):
                 acc[at, rows, :] += nt(g[j, xx], gate_f[at, :, chunk(j)]) + nt(u[j, xx], up_f[at, :, chunk(j)])
 
-        @pl.when(j == NC - 1)
-        def _():
-            for m in range(2):
-                for at in range(2):
-                    rows = pl.ds(pl.multiple_of((1 - core + 2 * m) * xb, xb), xb)
-                    dxs[at, m] = acc[at, rows, :].astype(BF)
-                    send(dxs.at[at, m], dxr.at[at, m], DXC + 2 * m + at, twin)
-
-        for i, (ref, theirs, own, out) in enumerate(((g, wgs, owg, gg_out), (u, wus, owu, gu_out))):
-            theirs[j] = column_grad(j, oh, ref)
-            send(theirs.at[j], out.at[:, cols(zh, j)], WX + 3 * j + 1 + i, partner)
-
-        for i, (ref, own, out) in enumerate(((g, owg, gg_out), (u, owu, gu_out))):
-            own[j] = column_grad(j, zh, ref)
-            keep(1 + i, own, out, (slice(None), cols(zh, j)), j)
-
     def row_grads(j):
-        got(halves(ht, j, x2, 0), HF + 2 * j)
-        got(halves(ht, j, x2, 1), HF + 2 * j + 1)
+        got(late(j, x2, 0), HF + 2 * j)
+        got(late(j, x2, 1), HF + 2 * j + 1)
         wds[j] = down_grad(j, oh)
         send(wds.at[j], gd_out.at[cols(zh, j), :], WX + 3 * j, partner)
         owd[j] = down_grad(j, zh)
         keep(0, owd, gd_out, (cols(zh, j),), j)
 
-    @pl.loop(0, NC + LAG)
+    @pl.loop(0, NC + 1)
     def _(i):
         @pl.when(i < NC)
         def _():
@@ -350,11 +377,28 @@
         def _():
             pl.loop(0, NC)(send_hidden)
 
-        @pl.when(i >= LAG)
+        @pl.when((i == NC - 1) | (i == NC))
         def _():
-            column_grads(i - LAG)
+            pl.loop(jnp.where(i == NC, 1, 0), jnp.where(i == NC, NC - 1, 1))(partner_columns)
+
+        @pl.when(i == NC)
+        def _():
+            pl.loop(0, NC - 1)(add_input_grad)
+
+    for i, ref in enumerate((g, u)):
+        got(halves(ref, NC - 1, x2, 0), AF + 4 * (NC - 1) + i)
+        got(halves(ref, NC - 1, x2, 1), AF + 4 * (NC - 1) + 2 + i)
+    add_input_grad(NC - 1)
+    for m in range(2):
+        for at in range(2):
+            rows = pl.ds(pl.multiple_of((1 - core + 2 * m) * xb, xb), xb)
+            dxs[at, m] = acc[at, rows, :].astype(BF)
+            send(dxs.at[at, m], dxr.at[at, m], DXC + 2 * m + at, twin)
+    send_columns(NC - 1)
 
     pl.loop(0, NC)(forward_hidden)
+    got(early(x2, 0), HE + 2)
+    got(early(x2, 1), HE + 3)
     for m in range(2):
         for at in range(2):
             got(dxr.at[at, m], DXC + 2 * m + at)
@@ -384,6 +428,7 @@
                 psend[d, step, rows, :] = total.astype(BF)
                 send(psend.at[d, step, rows], precv.at[d, step, rows], dx_sem(step, d, p), z_next if d == 0 else z_prev)
         if step >= 1:
+            own_columns(step - 1)
             row_grads(step - 1)
 
     for p in range(2):
@@ -394,6 +439,7 @@
             total = total + precv[d, 3, rows, :].astype(F32)
         fin[rows, :] = total.astype(BF)
         send(fin.at[rows], prev_out.at[rows], FIN + p, y_prev)
+    own_columns(NC - 1)
     row_grads(NC - 1)
     for p in range(2):
         got(prev_out.at[pl.ds(p * ht2, ht2)], FIN + p)
@@ -413,8 +459,8 @@
                 sent(ref.at[j, 0], AG + 4 * j + 2 * d + i)
                 sent(halves(ref, j, 0, 0), AF + 4 * j + 2 * d + i)
         for d in range(2):
-            sent(ht.at[j, 0], HA + 2 * j + d)
-            sent(halves(ht, j, 0, 0), HF + 2 * j + d)
+            sent(late(j, 0), HA + 2 * j + d)
+            sent(late(j, 0, 0), HF + 2 * j + d)
         mine = (gd_out.at[cols(zh, j), :], gg_out.at[:, cols(zh, j)], gu_out.at[:, cols(zh, j)])
         theirs = (gd_out.at[cols(oh, j), :], gg_out.at[:, cols(oh, j)], gu_out.at[:, cols(oh, j)])
         for i, (ref, own, out, arrived) in enumerate(zip((wds, wgs, wus), (owd, owg, owu), mine, theirs)):
@@ -422,6 +468,9 @@
             pltpu.make_async_copy(own.at[j], out, osem.at[j, i]).wait()
             got(arrived, WX + 3 * j + i)
 
+    for d in range(2):
+        sent(early(0), HE + d)
+        sent(early(0, 0), HE + 2 + d)
     for i in range(4):
         sent(dxs.at[0, 0], DXC + i)
     for step in range(4):

time: 153 us -> 149 us (0.974)
  Pallas kernels: 149 us -> 144 us
    pallas_call x1, Pallas kernels: 146 us -> 141 us  [shards(): pl.pallas_call(kernel, out_shape=(shape((tb, fb), BF), shape((fb, hb), BF...]
where the time goes in v3:
time: 149 us; the launch traced here: 148 us
  Pallas kernels  144 us (97%)
  local copies, waits for them, and re-layouts  2.56 us (2%)
    pallas_call x1, Pallas kernels, shards(): pl.pallas_call(kernel, out_shape=(shape((tb, fb), BF), shape((fb, hb), BF...  141 us

profile of v3, /device:TPU:8, one launch (start us, length us, event | category | flops | bytes accessed | tf_op | source)
XLA Modules:
  0.0 147.7 jit_solution(11704949653802890621)
XLA Ops:
  0.6 0.0 copy-start.5
  0.6 0.0 copy-start.4
  0.7 0.0 copy-start.3
  0.7 0.0 copy-start.8
  0.7 0.0 copy-start.7
  0.7 0.0 copy-start.6
  0.7 0.0 copy-start.2
  0.7 0.0 copy-start.1
  0.7 0.0 copy-start
  0.7 0.0 copy-start.9
  0.7 1.0 copy-done.9
  1.8 0.0 copy-start.10
  1.8 1.5 copy-done.10
  3.3 141.4 %relayed_gradients.1 = (bf16[256,256]{1,0:T(8,128)(2,1)S(1)}, bf16[256,1024]{1,0:T(8,128)(2,1)S(1)}, bf16[256,1024]{1,0:T(8,128)(2,1)S(1)}, bf16[1024,256]{1,0:T(8,128)(2,1)S(1)}) custom-call(bf16[1,256,256]{2,1,0:T(8,128)(2,1)S(1)} %copy-done.9, bf16[1,256,256]{2,1,0:T(8,128)(2,1)S(1)} %copy-done.10, bf16[1,256,1024]{2,1,0:T(8,128)(2,1)} %sg_in.1, ...), custom_call_target="tpu_custom_call" | custom-call | flops 6442450944 | bytes 12582912 | tf_op jit(solution)/shard_map/relayed_gradients/pallas_call | solution.py:542
  144.7 0.0 copy-done.5
  144.7 0.0 copy-done.4
  144.7 0.0 copy-done.3
  144.7 0.0 copy-done.8
  144.8 0.0 copy-done.7
  144.8 0.0 copy-done.6
  144.8 0.0 copy-done.2
  144.8 0.0 copy-done.1
  144.8 0.0 copy-done
  144.8 2.9 %sghmc_update.1 = (bf16[1,256,256]{2,1,0:T(8,128)(2,1)}, bf16[1,256,1024]{2,1,0:T(8,128)(2,1)}, bf16[1,256,1024]{2,1,0:T(8,128)(2,1)}, bf16[1,1024,256]{2,1,0:T(...) custom-call(bf16[256,256]{1,0:T(8,128)(2,1)S(1)} %get-tuple-element.11.prev, ...), custom_call_target="tpu_custom_call" | custom-call | tf_op jit(solution)/shard_map/sghmc_update/pallas_call | solution.py:564
Async XLA Ops:
  0.6 144.1 %copy-start.5 = (bf16[1,1024,256]{2,1,0:T(8,128)(2,1)S(1)}, bf16[1,1024,256]{2,1,0:T(8,128)(2,1)}, u32[]{:S(2)}) copy-start(bf16[1,1024,256]{2,1,0:T(8,128)(2,1)} %wd.1) | copy-start | bytes 1572868
  0.6 144.1 %copy-start.4 = (bf16[1,256,1024]{2,1,0:T(8,128)(2,1)S(1)}, bf16[1,256,1024]{2,1,0:T(8,128)(2,1)}, u32[]{:S(2)}) copy-start(bf16[1,256,1024]{2,1,0:T(8,128)(2,1)} %wu.1) | copy-start | bytes 1572868
  0.7 144.1 %copy-start.3 = (bf16[1,256,1024]{2,1,0:T(8,128)(2,1)S(1)}, bf16[1,256,1024]{2,1,0:T(8,128)(2,1)}, u32[]{:S(2)}) copy-start(bf16[1,256,1024]{2,1,0:T(8,128)(2,1)} %wg.1) | copy-start | bytes 1572868
  0.7 144.1 %copy-start.8 = (bf16[1,1024,256]{2,1,0:T(8,128)(2,1)S(1)}, bf16[1,1024,256]{2,1,0:T(8,128)(2,1)}, u32[]{:S(2)}) copy-start(bf16[1,1024,256]{2,1,0:T(8,128)(2,1)} %nd.1) | copy-start | bytes 1572868
  0.7 144.1 %copy-start.7 = (bf16[1,256,1024]{2,1,0:T(8,128)(2,1)S(1)}, bf16[1,256,1024]{2,1,0:T(8,128)(2,1)}, u32[]{:S(2)}) copy-start(bf16[1,256,1024]{2,1,0:T(8,128)(2,1)} %nu.1) | copy-start | bytes 1572868
  0.7 144.1 %copy-start.6 = (bf16[1,256,1024]{2,1,0:T(8,128)(2,1)S(1)}, bf16[1,256,1024]{2,1,0:T(8,128)(2,1)}, u32[]{:S(2)}) copy-start(bf16[1,256,1024]{2,1,0:T(8,128)(2,1)} %ng.1) | copy-start | bytes 1572868
  0.7 144.1 %copy-start.2 = (f32[1,1024,256]{2,1,0:T(8,128)S(1)}, f32[1,1024,256]{2,1,0:T(8,128)}, u32[]{:S(2)}) copy-start(f32[1,1024,256]{2,1,0:T(8,128)} %md.1) | copy-start | bytes 3145732
  0.7 144.1 %copy-start.1 = (f32[1,256,1024]{2,1,0:T(8,128)S(1)}, f32[1,256,1024]{2,1,0:T(8,128)}, u32[]{:S(2)}) copy-start(f32[1,256,1024]{2,1,0:T(8,128)} %mu.1) | copy-start | bytes 3145732
  0.7 144.1 %copy-start = (f32[1,256,1024]{2,1,0:T(8,128)S(1)}, f32[1,256,1024]{2,1,0:T(8,128)}, u32[]{:S(2)}) copy-start(f32[1,256,1024]{2,1,0:T(8,128)} %mg.1) | copy-start | bytes 3145732
  0.7 1.1 copy-start.9
  1.8 1.5 copy-start.10
